TPU v7x, 768 devices: a whole 4x8x12 slice. The times are simulated.
768 devices in a mesh: row: 16 (over y, core), col: 4 (over x), dep: 12 (over z).
Axes of the slice: x: 4, y: 8, z: 12, core: 2. Of those that a mesh axis runs over, the one named last changes fastest.
Arguments:
- b_tensor: bfloat16 [12, 24576, 3072], P(None, 'row', 'dep'), may hold values from -6 to 6
- occ_green: bfloat16 [3072, 512], P('dep', 'col'), may hold values from -0.15625 to 0.15625
- virt_green: bfloat16 [24576, 512], P('row'), may hold values from -0.0546875 to 0.0546875
- mu_atom: int32 [96], replicated, may hold values from 0 to 95, as said below
- mu_target: int32 [96], replicated, may hold values from 0 to 95, as said below
- mu_sizes: int32 [96], replicated, may hold values from 64 to 200, as said below
- nu_sizes: int32 [12], P('dep'), may hold values from 64 to 200, as said below
- screen: int32 [96, 12], P(None, 'dep'), may hold values 0 or 1
Outputs:
- second_mapping: float32 [512, 12, 512], P('row', 'dep', 'col')
Inputs may be any that keep to these rules, and one draw needn't show every extreme that they name: mu_target is a permutation of the block slots. Of the 6 slots a' with a' // 6 equal to one row index, at most 1 have target[a'] // 6 equal to one row index, and exactly 1 do for some such pair in every draw. mu_atom is a permutation of the atom blocks. `mu_sizes`: both ends are reached in every draw. `nu_sizes`: both ends are reached in every draw.
All inputs are finite; a program needn't handle non-finite values. No bound on the sum of `screen` on one device may be relied on, other than what follows from the above.
Results may differ from a plain program's by a relative error of at most 0.015.
Values may be sent and summed in bfloat16 or wider, within the bound.
A program may use at most 64 MiB of HBM per device.

v0:
```python
import jax
import jax.numpy as jnp
from jax import lax
from jax.sharding import PartitionSpec as P

BS = 256
NB_DEV = 6


def lookup(table, keys):
    equal = keys[:, None] == jnp.arange(table.shape[0], dtype=jnp.int32)[None, :]
    return jnp.sum(jnp.where(equal, table[None, :], 0), axis=1)


def body(b_tensor, occ_green, virt_green, mu_atom, mu_target, mu_sizes, nu_sizes, screen):
    slot_count = mu_atom.shape[0]
    rows_here = b_tensor.shape[1]
    first_slot = lax.axis_index("row") * NB_DEV
    inner = jnp.arange(BS, dtype=jnp.int32)
    local_atoms = lax.dynamic_slice_in_dim(mu_atom, first_slot, NB_DEV, 0)
    mu_len = lookup(mu_sizes, local_atoms)
    row_keep = (inner[None, :] < mu_len[:, None]).astype(jnp.bfloat16)
    col_keep = (inner[None, :] < nu_sizes[:, None]).astype(jnp.bfloat16)
    atom_hits = (local_atoms[:, None] == jnp.arange(slot_count, dtype=jnp.int32)[None, :]).astype(
        jnp.bfloat16
    )
    block_keep = jnp.dot(
        atom_hits, screen.astype(jnp.bfloat16), preferred_element_type=jnp.float32
    ).astype(jnp.bfloat16)
    keep = row_keep[:, :, None, None] * block_keep[:, None, :, None] * col_keep[None, None, :, :]
    masked = b_tensor * keep.reshape(rows_here, b_tensor.shape[2])[None]
    aux_here = b_tensor.shape[0] // lax.axis_size("dep")
    flat = masked.reshape(aux_here * lax.axis_size("dep") * rows_here, masked.shape[2])
    product = jnp.dot(flat, occ_green, preferred_element_type=jnp.float32)
    first = lax.psum_scatter(
        product.reshape(aux_here * lax.axis_size("dep"), rows_here, occ_green.shape[1]).astype(
            jnp.bfloat16
        ),
        "dep",
        scatter_dimension=0,
        tiled=True,
    )
    blocks = first.reshape(aux_here, NB_DEV, BS, first.shape[2]).transpose(1, 0, 2, 3)
    all_target = lookup(mu_target, mu_atom)
    mine = (
        all_target[:, None] - first_slot == jnp.arange(NB_DEV, dtype=jnp.int32)[None, :]
    ).astype(jnp.bfloat16)
    chosen = jnp.einsum(
        "kj,kpbl->jpbl",
        mine,
        lax.all_gather(blocks, "row", axis=0, tiled=True),
        preferred_element_type=jnp.float32,
    )
    chosen = chosen.astype(jnp.bfloat16)
    green_blocks = virt_green.reshape(NB_DEV, BS, virt_green.shape[1])
    return lax.psum_scatter(
        jnp.einsum("jbs,jpbl->spl", green_blocks, chosen, preferred_element_type=jnp.float32),
        "row",
        scatter_dimension=0,
        tiled=True,
    )


def solution(mesh):
    placed = (
        P(None, "row", "dep"),
        P("dep", "col"),
        P("row", None),
        P(),
        P(),
        P(),
        P("dep"),
        P(None, "dep"),
    )
    return jax.shard_map(
        body, mesh=mesh, in_specs=placed, out_specs=P("row", "dep", "col"), check_vma=False
    )
```

profile of v0, /device:TPU:1, one launch (start us, length us, event | category | flops | bytes accessed | tf_op | source)
XLA Modules:
  0.0 222.4 jit_solution(4454955109743785335)
XLA Ops:
  6.5 0.0 copy-start
  6.5 0.0 reduce-scatter.3.cloned.1.call-start
  7.3 0.7 dynamic_slice.3
  8.1 0.8 select_reduce_fusion.1
  8.9 0.8 fusion.12
  9.7 0.1 fusion.15
  9.8 0.3 broadcast_multiply_fusion
  10.1 0.0 copy-start.1
  10.1 0.0 copy-start.2
  10.1 8.4 %fusion.6 = bf16[12,1536,128]{2,1,0:T(8,128)(2,1)} fusion(bf16[12,1536,256]{2,1,0:T(8,128)(2,1)} %param.8, bf16[1536,256]{1,0:T(8,128)(2,1)S(1)} %broadcast_multiply_fusion, bf16[256,128]{1,0:T(8,128)(2,1)} %param.9), kind=kOutput, calls=%fused_computation.6 | convolution fusion | flops 1215037440 | bytes 15007744 | tf_op jit(solution)/shard_map/dot_general | solution.py:34
  18.6 0.0 reduce-scatter.3.cloned.1.call-update
  18.6 0.0 all-gather.2.cloned.1.call-start
  18.6 74.7 %reduce-scatter.3.cloned.1.call-done = bf16[1,1536,128]{2,1,0:T(8,128)(2,1)} async-done(((bf16[12,1536,128]{2,1,0:T(8,128)(2,1)}), bf16[1,1536,128]{2,1,0:T(8,128)(2,1)}) %reduce-scatter.3.cloned.1.call-update) | async-done | bytes 393232 | tf_op jit(solution)/shard_map/reduce_scatter | solution.py:35
  93.3 0.0 all-gather.2.cloned.1.call-update
  93.3 0.0 reduce-scatter.5.cloned.1.call-start
  93.4 0.0 copy-done.1
  93.4 0.0 copy-done.2
  93.4 0.2 select_reduce_fusion
  93.6 56.0 %all-gather.2.cloned.1.call-done = bf16[96,1,256,128]{3,2,1,0:T(8,128)(2,1)} async-done(((bf16[6,1,256,128]{3,2,1,0:T(8,128)(2,1)}), bf16[96,1,256,128]{3,2,1,0:T(8,128)(2,1)}) %all-gather.2.cloned.1.call-update) | async-done | bytes 6291472 | tf_op jit(solution)/shard_map/all_gather | solution.py:51
  149.6 6.2 %fusion.9 = bf16[6,256,128]{2,0,1:T(8,128)(2,1)S(1)} fusion(bf16[96,1,256,128]{3,2,1,0:T(8,128)(2,1)} %all-gather.2.cloned.1.call-done, s32[96]{0:T(128)S(1)} %broadcast_subtract_fusion), kind=kOutput, calls=%fused_computation.7 | convolution fusion | flops 37945920 | bytes 6685056 | tf_op jit(solution)/shard_map/kj,kpbl->jpbl/dot_general | solution.py:48
  155.8 0.0 copy-done
  155.8 0.4 convolution_bitcast_fusion
  156.2 0.8 copy.15
  157.0 0.0 reduce-scatter.5.cloned.1.call-update
  157.0 58.8 %reduce-scatter.5.cloned.1.call-done = f32[32,1,128]{2,1,0:T(1,128)} async-done(((f32[512,1,128]{2,1,0:T(1,128)}), f32[32,1,128]{2,1,0:T(1,128)}) %reduce-scatter.5.cloned.1.call-update) | async-done | bytes 16400 | tf_op jit(solution)/shard_map/reduce_scatter | solution.py:56
  (3 shorter events, 0.0 us)
Async XLA Ops:
  6.5 149.2 %copy-start = (bf16[1536,512]{1,0:T(8,128)(2,1)S(1)}, bf16[1536,512]{1,0:T(8,128)(2,1)}, u32[]{:S(2)}) copy-start(bf16[1536,512]{1,0:T(8,128)(2,1)} %param.10) | copy-start | bytes 4718596
  6.5 86.8 %reduce-scatter.3.cloned.1.call-start = ((), (), s32[]{:S(2)}) async-start(), calls=%async_computation.2 | async-start | bytes 5111808 | tf_op jit(solution)/shard_map/reduce_scatter | solution.py:35
  10.1 83.3 %copy-start.1 = (s32[96]{0:T(128)S(1)}, s32[96]{0:T(128)}, u32[]{:S(2)}) copy-start(s32[96]{0:T(128)} %param.11) | copy-start | bytes 1156
  10.1 83.3 %copy-start.2 = (s32[96]{0:T(128)S(1)}, s32[96]{0:T(128)}, u32[]{:S(2)}) copy-start(s32[96]{0:T(128)} %param.12) | copy-start | bytes 1156
  18.6 131.0 %all-gather.2.cloned.1.call-start = ((), (), s32[]{:S(2)}) async-start(), calls=%async_computation.3 | async-start | bytes 6684672 | tf_op jit(solution)/shard_map/all_gather | solution.py:51
  93.3 122.6 %reduce-scatter.5.cloned.1.call-start = ((), (), s32[]{:S(2)}) async-start(), calls=%async_computation.4 | async-start | bytes 278528 | tf_op jit(solution)/shard_map/reduce_scatter | solution.py:56
Sparse Core Ops, SparseCore 0:
  18.7 74.5 reduce-scatter.2
  95.7 53.8 all-gather.1
  157.2 58.6 reduce-scatter.4
where the time goes:
time: 223 us; the launch traced here: 222 us
  waiting for transfers between devices  190 us (85%)
  matrix products  15.9 us (7%)
  between operations  13.9 us (6%)
    reduce_scatter x1, waiting for transfers between devices, body(): lax.psum_scatter(product.reshape(aux_here * lax.axis_size('dep'), rows_he...  74.7 us
    reduce_scatter x1, waiting for transfers between devices, body(): lax.psum_scatter(jnp.einsum('jbs,jpbl->spl', green_blocks, chosen, prefer...  58.8 us
    all_gather x1, waiting for transfers between devices, body(): lax.all_gather(blocks, 'row', axis=0, tiled=True)  56 us
    dot_general x1, matrix products, body(): product = jnp.dot(flat, occ_green, preferred_element_type=jnp.float32)  8.44 us
    dot_general x1, matrix products, body(): jnp.einsum('kj,kpbl->jpbl', mine, lax.all_gather(blocks, 'row', axis=0, t...  6.18 us
  transfers between devices with their start and end apart: 3, of which 3 were waited for; matrix products, arithmetic and copies ran while one was open for 0% of the time, Pallas kernels for 0%

commit v1 on v0

v1 whole, which is shorter than its diff:
```python
import functools

import jax
import jax.numpy as jnp
from jax import lax
from jax.experimental import pallas as pl
from jax.experimental.pallas import tpu as pltpu
from jax.sharding import PartitionSpec as P

MESH = pl.DeviceIdType.MESH
BF16 = jnp.bfloat16
F32 = jnp.float32

BS = 256
NB = 6
KEPT = 208
NROW, NCOL, NDEP = 16, 4, 12
NY = NROW // 2
NP = 12
SIG = 512
GROUPS = 3
P_GROUP = NP // GROUPS
ROWS_GROUP = P_GROUP * 8


def wrap(value, size):
    return jnp.where(value >= size, value - size, value)


def kernel(
    atom_ref,
    target_ref,
    size_ref,
    nu_ref,
    screen_ref,
    b_ref,
    virt_ref,
    occ_ref,
    out_ref,
    b_buf,
    virt_buf,
    occ_buf,
    picked,
    green_out,
    green_in,
    y_buf,
    y_pair,
    y_out,
    y_in,
    w_out,
    w_in,
    x_out,
    b_sem,
    local_sem,
    green_send,
    green_recv,
    occ_send,
    occ_recv,
    pair_send,
    pair_recv,
    y_send,
    y_recv,
    w_send,
    w_recv,
    x_send,
    x_recv,
):
    row, col, dep = lax.axis_index("row"), lax.axis_index("col"), lax.axis_index("dep")
    core = lax.rem(row, 2)
    y = lax.div(row, 2)
    other = 1 - core

    virt_copy = pltpu.make_async_copy(virt_ref.at[:, pl.ds(0, KEPT), :], virt_buf, local_sem.at[0])
    virt_copy.start()
    mine = pl.multiple_of(col * 128, 128)
    occ_copy = pltpu.make_async_copy(occ_ref, occ_buf.at[:, pl.ds(mine, 128)], local_sem.at[1])
    occ_copy.start()
    b_copies = [
        pltpu.make_async_copy(b_ref.at[p, :, pl.ds(0, KEPT), :], b_buf.at[p], b_sem.at[p]) for p in range(NP)
    ]
    for copy in b_copies:
        copy.start()

    rows_of = [wrap(row + o, NROW) for o in range(NROW)]
    ys_of = [wrap(y + o, NY) for o in range(NY)]
    cols_of = [wrap(col + o, NCOL) for o in range(NCOL)]
    deps_of = [wrap(dep + o, NDEP) for o in range(NDEP)]
    barrier = pltpu.get_barrier_semaphore()
    for o in range(1, NDEP):
        pl.semaphore_signal(barrier, inc=1, device_id=(row, col, deps_of[o]), device_id_type=MESH)
    for o in range(1, NROW):
        pl.semaphore_signal(barrier, inc=1, device_id=(rows_of[o], col, dep), device_id_type=MESH)
    for o in range(1, NCOL):
        pl.semaphore_signal(barrier, inc=1, device_id=(row, cols_of[o], dep), device_id_type=MESH)

    q = lax.broadcasted_iota(jnp.int32, (SIG, 128), 1)
    owner = 2 * ((q // 8) % 8) + q // 64
    column = owner * 32 + col * 8 + q % 8
    choose = jnp.where(lax.broadcasted_iota(jnp.int32, (SIG, 128), 0) == column, 1.0, 0.0).astype(BF16)
    virt_copy.wait()
    picked[...] = (
        jnp.dot(virt_buf[...].reshape(NB * KEPT, SIG), choose, preferred_element_type=F32)
        .astype(BF16)
        .reshape(NB, KEPT, 128)
    )

    first = row * NB
    for o in range(NROW):
        wanted = jnp.int32(0)
        for j in range(NB):
            t = target_ref[atom_ref[rows_of[o] * NB + j]] - first
            wanted += jnp.where((t >= 0) & (t < NB), t, 0)
        if o == 0:
            green_in[row] = picked[wanted]
        else:
            green_out[o] = picked[wanted]

    pl.semaphore_wait(barrier, NDEP + NROW + NCOL - 3)

    green_copies = []
    for o in (8, 9, 7, 10, 6, 11, 5, 12, 4, 13, 3, 14, 2, 15, 1):
        copy = pltpu.make_async_remote_copy(
            green_out.at[o], green_in.at[row], green_send.at[o], green_recv.at[row],
            device_id=(rows_of[o], col, dep), device_id_type=MESH,
        )
        copy.start()
        green_copies.append(copy)
    occ_copy.wait()
    occ_copies = []
    for o in range(1, NCOL):
        copy = pltpu.make_async_remote_copy(
            occ_buf.at[:, pl.ds(mine, 128)], occ_buf.at[:, pl.ds(mine, 128)], occ_send.at[o], occ_recv.at[col],
            device_id=(row, cols_of[o], dep), device_id_type=MESH,
        )
        copy.start()
        occ_copies.append(copy)

    def arrived(ref, send, recv):
        pltpu.make_async_copy(ref, ref, recv).wait()

    for o in range(1, NROW):
        arrived(green_in.at[rows_of[o]], None, green_recv.at[rows_of[o]])

    parts = []
    for j in range(NB):
        atom = atom_ref[row * NB + j]
        source = target_ref[atom] // NB
        kept = size_ref[atom] * screen_ref[atom]
        inside = lax.broadcasted_iota(jnp.int32, (KEPT, 128), 0) < kept
        parts.append(jnp.where(inside, green_in[source].astype(F32), 0.0).astype(BF16))
    rows_first = jnp.concatenate(parts, axis=0)
    eye = jnp.where(
        lax.broadcasted_iota(jnp.int32, (128, 128), 0) == lax.broadcasted_iota(jnp.int32, (128, 128), 1), 1.0, 0.0
    ).astype(BF16)
    green = lax.dot_general(eye, rows_first, (((1,), (1,)), ((), ())), preferred_element_type=F32).astype(BF16)

    pair_copies = []
    for g in range(GROUPS):
        for h in range(P_GROUP // 2):
            halves = []
            for k in range(2):
                p = g * P_GROUP + 2 * h + k
                b_copies[p].wait()
                block = b_buf[p].reshape(NB * KEPT, BS)
                halves.append(jnp.dot(green, block, preferred_element_type=F32).reshape(2, NY, 8, BS))
            y_buf[g, :, :, pl.ds(h * 16, 16), :] = jnp.concatenate(halves, axis=2).astype(BF16)
        copy = pltpu.make_async_remote_copy(
            y_buf.at[g, other], y_pair.at[g], pair_send.at[g], pair_recv.at[g],
            device_id=(row + 1 - 2 * core, col, dep), device_id_type=MESH,
        )
        copy.start()
        pair_copies.append(copy)

    y_copies = []
    for g in range(GROUPS):
        pair_copies[g].wait_recv()
        y_out[g] = (y_buf[g, core].astype(F32) + y_pair[g].astype(F32)).astype(BF16)
        for o in (4, 5, 3, 6, 2, 7, 1):
            copy = pltpu.make_async_remote_copy(
                y_out.at[g, ys_of[o]], y_in.at[g, y], y_send.at[g, o], y_recv.at[g, y],
                device_id=(2 * ys_of[o] + core, col, dep), device_id_type=MESH,
            )
            copy.start()
            y_copies.append(copy)
        y_in[g, y] = y_out[g, y]

    for o in range(1, NCOL):
        piece = occ_buf.at[:, pl.ds(pl.multiple_of(cols_of[o] * 128, 128), 128)]
        arrived(piece, None, occ_recv.at[cols_of[o]])
    occ_kept = lax.broadcasted_iota(jnp.int32, (BS, SIG), 0) < nu_ref[0]
    occ = jnp.where(occ_kept, occ_buf[...].astype(F32), 0.0).astype(BF16)

    for g in range(GROUPS):
        for o in range(1, NY):
            arrived(y_in.at[g, ys_of[o]], None, y_recv.at[g, ys_of[o]])
        total = y_in[g, 0].astype(F32)
        for k in range(1, NY):
            total += y_in[g, k].astype(F32)
        w = jnp.dot(total.astype(BF16), occ, preferred_element_type=F32)
        for k in range(P_GROUP):
            p = g * P_GROUP + k
            mine_w = w[k * 8 : (k + 1) * 8]
            w_out[p] = jnp.concatenate([mine_w[:, :256], mine_w[:, 256:]], axis=0).astype(BF16)

            @pl.when(dep != p)
            def _():
                pltpu.make_async_remote_copy(
                    w_out.at[p], w_in.at[dep], w_send.at[p], w_recv.at[dep],
                    device_id=(row, col, p), device_id_type=MESH,
                ).start()

    w_in[dep] = w_out[dep]
    for o in range(1, NDEP):
        arrived(w_in.at[deps_of[o]], None, w_recv.at[deps_of[o]])
    result = w_in[0].astype(F32)
    for k in range(1, NDEP):
        result += w_in[k].astype(F32)
    for c in range(NCOL):
        x_out[c] = result[(c // 2) * 8 : (c // 2) * 8 + 8, (c % 2) * 128 : (c % 2) * 128 + 128]
    x_copies = []
    for o in range(1, NCOL):
        copy = pltpu.make_async_remote_copy(
            x_out.at[cols_of[o]], out_ref.at[col], x_send.at[o], x_recv.at[col],
            device_id=(row, cols_of[o], dep), device_id_type=MESH,
        )
        copy.start()
        x_copies.append(copy)
    out_ref[col] = x_out[col]

    for copy in green_copies + occ_copies + pair_copies + y_copies:
        copy.wait_send()
    for o in range(1, NDEP):
        d = deps_of[o]
        pltpu.make_async_copy(w_out.at[d], w_out.at[d], w_send.at[d]).wait()
    for copy in x_copies:
        copy.wait_send()
    for o in range(1, NCOL):
        arrived(out_ref.at[cols_of[o]], None, x_recv.at[cols_of[o]])


def body(b_tensor, occ_green, virt_green, mu_atom, mu_target, mu_sizes, nu_sizes, screen):
    smem = pl.BlockSpec(memory_space=pltpu.SMEM)
    hbm = pl.BlockSpec(memory_space=pl.ANY)
    dma = pltpu.SemaphoreType.DMA
    out = pl.pallas_call(
        kernel,
        name="contract",
        out_shape=jax.ShapeDtypeStruct((NCOL, 8, 128), F32),
        in_specs=[smem] * 5 + [hbm] * 3,
        out_specs=pl.BlockSpec(memory_space=pltpu.VMEM),
        scratch_shapes=[
            pltpu.VMEM((NP, NB, KEPT, BS), BF16),
            pltpu.VMEM((NB, KEPT, SIG), BF16),
            pltpu.VMEM((BS, SIG), BF16),
            pltpu.VMEM((NB, KEPT, 128), BF16),
            pltpu.VMEM((NROW, KEPT, 128), BF16),
            pltpu.VMEM((NROW, KEPT, 128), BF16),
            pltpu.VMEM((GROUPS, 2, NY, ROWS_GROUP, BS), BF16),
            pltpu.VMEM((GROUPS, NY, ROWS_GROUP, BS), BF16),
            pltpu.VMEM((GROUPS, NY, ROWS_GROUP, BS), BF16),
            pltpu.VMEM((GROUPS, NY, ROWS_GROUP, BS), BF16),
            pltpu.VMEM((NP, 16, 256), BF16),
            pltpu.VMEM((NDEP, 16, 256), BF16),
            pltpu.VMEM((NCOL, 8, 128), F32),
            dma((NP,)),
            dma((2,)),
            dma((NROW,)),
            dma((NROW,)),
            dma((NCOL,)),
            dma((NCOL,)),
            dma((GROUPS,)),
            dma((GROUPS,)),
            dma((GROUPS, NY)),
            dma((GROUPS, NY)),
            dma((NP,)),
            dma((NDEP,)),
            dma((NCOL,)),
            dma((NCOL,)),
        ],
        compiler_params=pltpu.CompilerParams(
            collective_id=0, has_side_effects=True, vmem_limit_bytes=56 * 2**20
        ),
        cost_estimate=pl.CostEstimate(flops=1700000000, bytes_accessed=10000000, transcendentals=0),
    )(
        mu_atom,
        mu_target,
        mu_sizes,
        nu_sizes,
        screen.reshape(screen.shape[0]),
        b_tensor.reshape(NP, NB, BS, BS),
        virt_green.reshape(NB, BS, SIG),
        occ_green,
    )
    return out.reshape(SIG // NROW, 1, 128)


def solution(mesh):
    placed = (
        P(None, "row", "dep"),
        P("dep", "col"),
        P("row", None),
        P(),
        P(),
        P(),
        P("dep"),
        P(None, "dep"),
    )
    return jax.shard_map(
        body, mesh=mesh, in_specs=placed, out_specs=P("row", "dep", "col"), check_vma=False
    )
```

time: 223 us -> 63.1 us (0.28)
  the two profiles are of different devices: /device:TPU:1 before, /device:TPU:8 now
where the time goes in v1:
time: 63.1 us; the launch traced here: 62.9 us
  Pallas kernels  60.9 us (97%)
  local copies, waits for them, and re-layouts  1.32 us (2%)
  between operations  0.66 us (1%)
    pallas_call x1, Pallas kernels, body(): pl.pallas_call(kernel, name='contract', out_shape=jax.ShapeDtypeStruct((N...  60.9 us
    unnamed x1, local copies, waits for them, and re-layouts  1.32 us

profile of v1, /device:TPU:8, one launch (start us, length us, event | category | flops | bytes accessed | tf_op | source)
XLA Modules:
  0.0 62.9 jit_solution(10468672400603056376)
XLA Ops:
  0.7 60.9 %contract.1 = f32[4,8,128]{2,1,0:T(8,128)} custom-call(s32[96]{0:T(128)} %atom_ref.1, s32[96]{0:T(128)} %target_ref.1, s32[96]{0:T(128)} %size_ref.1, s32[1]{0:T(128)S(6)} %copy.11.nu_ref, s32[96]{0:T(128)} %bitcast.9, bf16[12,6,256,256]{3,2,1,0:T(8,128)(2,1)} %bitcast.6, bf16[6,256,512]{2,1,0:T(8,128)(2,1)} %bitcast.7, bf16[256,128]{1,0:T(8,128)(2,1)} %occ_ref.1), custom_call_target="tpu_custom_call" | custom-call | flops 1700000000 | bytes 10000000 | tf_op jit(solution)/shard_map/contract/pallas_call | solution.py:245
  61.6 1.3 %copy.12 = f32[32,1,128]{2,1,0:T(1,128)} copy(f32[32,1,128]{2,1,0:T(1,128)} %bitcast.8) | data formatting | bytes 32768

commit v2 on v1

v2 whole, which is shorter than its diff:
```python
import functools

import jax
import jax.numpy as jnp
from jax import lax
from jax.experimental import pallas as pl
from jax.experimental.pallas import tpu as pltpu
from jax.sharding import PartitionSpec as P

MESH = pl.DeviceIdType.MESH
BF16 = jnp.bfloat16
F32 = jnp.float32

BS = 256
NB = 6
KEPT = 208
NROW, NCOL, NDEP = 16, 4, 12
NY = NROW // 2
NP = 12
SIG = 512
GROUPS = 3
P_GROUP = NP // GROUPS
ROWS_GROUP = P_GROUP * 8


def wrap(value, size):
    return jnp.where(value >= size, value - size, value)


def kernel(
    atom_ref,
    target_ref,
    size_ref,
    nu_ref,
    screen_ref,
    b_ref,
    virt_ref,
    occ_ref,
    out_ref,
    b_buf,
    virt_buf,
    occ_buf,
    picked,
    green_out,
    green_in,
    y_buf,
    y_pair,
    y_out,
    y_in,
    w_out,
    w_in,
    x_out,
    b_sem,
    local_sem,
    green_send,
    green_recv,
    occ_send,
    occ_recv,
    pair_send,
    pair_recv,
    y_send,
    y_recv,
    w_send,
    w_recv,
    x_send,
    x_recv,
):
    row, col, dep = lax.axis_index("row"), lax.axis_index("col"), lax.axis_index("dep")
    core = lax.rem(row, 2)
    y = lax.div(row, 2)
    other = 1 - core

    virt_copy = pltpu.make_async_copy(virt_ref.at[:, pl.ds(0, KEPT), :], virt_buf, local_sem.at[0])
    virt_copy.start()
    mine = pl.multiple_of(col * 128, 128)
    occ_copy = pltpu.make_async_copy(occ_ref, occ_buf.at[:, pl.ds(mine, 128)], local_sem.at[1])
    occ_copy.start()
    b_copies = [
        pltpu.make_async_copy(b_ref.at[p, :, pl.ds(0, KEPT), :], b_buf.at[p], b_sem.at[p]) for p in range(NP)
    ]

    rows_of = [wrap(row + o, NROW) for o in range(NROW)]
    ys_of = [wrap(y + o, NY) for o in range(NY)]
    cols_of = [wrap(col + o, NCOL) for o in range(NCOL)]
    deps_of = [wrap(dep + o, NDEP) for o in range(NDEP)]
    barrier = pltpu.get_barrier_semaphore()
    for o in range(1, NDEP):
        pl.semaphore_signal(barrier, inc=1, device_id=(row, col, deps_of[o]), device_id_type=MESH)
    for o in range(1, NROW):
        pl.semaphore_signal(barrier, inc=1, device_id=(rows_of[o], col, dep), device_id_type=MESH)
    for o in range(1, NCOL):
        pl.semaphore_signal(barrier, inc=1, device_id=(row, cols_of[o], dep), device_id_type=MESH)

    with jax.named_scope("pick"):
        q = lax.broadcasted_iota(jnp.int32, (SIG, 128), 1)
        owner = 2 * ((q // 8) % 8) + q // 64
        column = owner * 32 + col * 8 + q % 8
        choose = jnp.where(lax.broadcasted_iota(jnp.int32, (SIG, 128), 0) == column, 1.0, 0.0).astype(BF16)
        virt_copy.wait()
        for copy in b_copies:
            copy.start()
        picked[...] = (
            jnp.dot(virt_buf[...].reshape(NB * KEPT, SIG), choose, preferred_element_type=F32)
            .astype(BF16)
            .reshape(NB, KEPT, 128)
        )

        first = row * NB
        for o in range(NROW):
            wanted = jnp.int32(0)
            for j in range(NB):
                t = target_ref[atom_ref[rows_of[o] * NB + j]] - first
                wanted += jnp.where((t >= 0) & (t < NB), t, 0)
            if o == 0:
                green_in[row] = picked[wanted]
            else:
                green_out[o] = picked[wanted]

    with jax.named_scope("barrier"):
        pl.semaphore_wait(barrier, NDEP + NROW + NCOL - 3)

    with jax.named_scope("green_send"):
        green_copies = []
        for o in (8, 9, 7, 10, 6, 11, 5, 12, 4, 13, 3, 14, 2, 15, 1):
            copy = pltpu.make_async_remote_copy(
                green_out.at[o], green_in.at[row], green_send.at[o], green_recv.at[row],
                device_id=(rows_of[o], col, dep), device_id_type=MESH,
            )
            copy.start()
            green_copies.append(copy)
        occ_copy.wait()
        occ_copies = []
        for o in range(1, NCOL):
            copy = pltpu.make_async_remote_copy(
                occ_buf.at[:, pl.ds(mine, 128)], occ_buf.at[:, pl.ds(mine, 128)], occ_send.at[o], occ_recv.at[col],
                device_id=(row, cols_of[o], dep), device_id_type=MESH,
            )
            copy.start()
            occ_copies.append(copy)

    def arrived(ref, send, recv):
        pltpu.make_async_copy(ref, ref, recv).wait()

    with jax.named_scope("green_wait"):
        for o in range(1, NROW):
            arrived(green_in.at[rows_of[o]], None, green_recv.at[rows_of[o]])

    with jax.named_scope("green_mask"):
        parts = []
        for j in range(NB):
            atom = atom_ref[row * NB + j]
            source = target_ref[atom] // NB
            kept = size_ref[atom] * screen_ref[atom]
            inside = lax.broadcasted_iota(jnp.int32, (KEPT, 128), 0) < kept
            parts.append(jnp.where(inside, green_in[source].astype(F32), 0.0).astype(BF16))
        rows_first = jnp.concatenate(parts, axis=0)
        eye = jnp.where(
            lax.broadcasted_iota(jnp.int32, (128, 128), 0) == lax.broadcasted_iota(jnp.int32, (128, 128), 1), 1.0, 0.0
        ).astype(BF16)
        green = lax.dot_general(eye, rows_first, (((1,), (1,)), ((), ())), preferred_element_type=F32).astype(BF16)

    with jax.named_scope("y_dot"):
        pair_copies = []
        for g in range(GROUPS):
            for h in range(P_GROUP // 2):
                halves = []
                for k in range(2):
                    p = g * P_GROUP + 2 * h + k
                    b_copies[p].wait()
                    block = b_buf[p].reshape(NB * KEPT, BS)
                    halves.append(jnp.dot(green, block, preferred_element_type=F32).reshape(2, NY, 8, BS))
                y_buf[g, :, :, pl.ds(h * 16, 16), :] = jnp.concatenate(halves, axis=2).astype(BF16)
            copy = pltpu.make_async_remote_copy(
                y_buf.at[g, other], y_pair.at[g], pair_send.at[g], pair_recv.at[g],
                device_id=(row + 1 - 2 * core, col, dep), device_id_type=MESH,
            )
            copy.start()
            pair_copies.append(copy)

    with jax.named_scope("pair_sum"):
        y_copies = []
        for g in range(GROUPS):
            pair_copies[g].wait_recv()
            y_out[g] = (y_buf[g, core].astype(F32) + y_pair[g].astype(F32)).astype(BF16)
            for o in (4, 5, 3, 6, 2, 7, 1):
                copy = pltpu.make_async_remote_copy(
                    y_out.at[g, ys_of[o]], y_in.at[g, y], y_send.at[g, o], y_recv.at[g, y],
                    device_id=(2 * ys_of[o] + core, col, dep), device_id_type=MESH,
                )
                copy.start()
                y_copies.append(copy)
            y_in[g, y] = y_out[g, y]

    for o in range(1, NCOL):
        piece = occ_buf.at[:, pl.ds(pl.multiple_of(cols_of[o] * 128, 128), 128)]
        arrived(piece, None, occ_recv.at[cols_of[o]])
    occ_kept = lax.broadcasted_iota(jnp.int32, (BS, SIG), 0) < nu_ref[0]
    occ = jnp.where(occ_kept, occ_buf[...].astype(F32), 0.0).astype(BF16)

    with jax.named_scope("y_sum"):
        for g in range(GROUPS):
            for o in range(1, NY):
                arrived(y_in.at[g, ys_of[o]], None, y_recv.at[g, ys_of[o]])
            total = y_in[g, 0].astype(F32)
            for k in range(1, NY):
                total += y_in[g, k].astype(F32)
            w = jnp.dot(total.astype(BF16), occ, preferred_element_type=F32)
            for k in range(P_GROUP):
                p = g * P_GROUP + k
                mine_w = w[k * 8 : (k + 1) * 8]
                w_out[p] = jnp.concatenate([mine_w[:, :256], mine_w[:, 256:]], axis=0).astype(BF16)

                @pl.when(dep != p)
                def _():
                    pltpu.make_async_remote_copy(
                        w_out.at[p], w_in.at[dep], w_send.at[p], w_recv.at[dep],
                        device_id=(row, col, p), device_id_type=MESH,
                    ).start()

    with jax.named_scope("w_sum"):
        w_in[dep] = w_out[dep]
        for o in range(1, NDEP):
            arrived(w_in.at[deps_of[o]], None, w_recv.at[deps_of[o]])
        result = w_in[0].astype(F32)
        for k in range(1, NDEP):
            result += w_in[k].astype(F32)
        for c in range(NCOL):
            x_out[c] = result[(c // 2) * 8 : (c // 2) * 8 + 8, (c % 2) * 128 : (c % 2) * 128 + 128]
    with jax.named_scope("x_end"):
        x_copies = []
        for o in range(1, NCOL):
            copy = pltpu.make_async_remote_copy(
                x_out.at[cols_of[o]], out_ref.at[col], x_send.at[o], x_recv.at[col],
                device_id=(row, cols_of[o], dep), device_id_type=MESH,
            )
            copy.start()
            x_copies.append(copy)
        out_ref[col] = x_out[col]

        for copy in green_copies + occ_copies + pair_copies + y_copies:
            copy.wait_send()
        for o in range(1, NDEP):
            d = deps_of[o]
            pltpu.make_async_copy(w_out.at[d], w_out.at[d], w_send.at[d]).wait()
        for copy in x_copies:
            copy.wait_send()
        for o in range(1, NCOL):
            arrived(out_ref.at[cols_of[o]], None, x_recv.at[cols_of[o]])


def body(b_tensor, occ_green, virt_green, mu_atom, mu_target, mu_sizes, nu_sizes, screen):
    smem = pl.BlockSpec(memory_space=pltpu.SMEM)
    hbm = pl.BlockSpec(memory_space=pl.ANY)
    dma = pltpu.SemaphoreType.DMA
    out = pl.pallas_call(
        kernel,
        name="contract",
        out_shape=jax.ShapeDtypeStruct((NCOL, 8, 128), F32),
        in_specs=[smem] * 5 + [hbm] * 3,
        out_specs=pl.BlockSpec(memory_space=pltpu.VMEM),
        scratch_shapes=[
            pltpu.VMEM((NP, NB, KEPT, BS), BF16),
            pltpu.VMEM((NB, KEPT, SIG), BF16),
            pltpu.VMEM((BS, SIG), BF16),
            pltpu.VMEM((NB, KEPT, 128), BF16),
            pltpu.VMEM((NROW, KEPT, 128), BF16),
            pltpu.VMEM((NROW, KEPT, 128), BF16),
            pltpu.VMEM((GROUPS, 2, NY, ROWS_GROUP, BS), BF16),
            pltpu.VMEM((GROUPS, NY, ROWS_GROUP, BS), BF16),
            pltpu.VMEM((GROUPS, NY, ROWS_GROUP, BS), BF16),
            pltpu.VMEM((GROUPS, NY, ROWS_GROUP, BS), BF16),
            pltpu.VMEM((NP, 16, 256), BF16),
            pltpu.VMEM((NDEP, 16, 256), BF16),
            pltpu.VMEM((NCOL, 8, 128), F32),
            dma((NP,)),
            dma((2,)),
            dma((NROW,)),
            dma((NROW,)),
            dma((NCOL,)),
            dma((NCOL,)),
            dma((GROUPS,)),
            dma((GROUPS,)),
            dma((GROUPS, NY)),
            dma((GROUPS, NY)),
            dma((NP,)),
            dma((NDEP,)),
            dma((NCOL,)),
            dma((NCOL,)),
        ],
        compiler_params=pltpu.CompilerParams(
            collective_id=0, has_side_effects=True, vmem_limit_bytes=56 * 2**20
        ),
        cost_estimate=pl.CostEstimate(flops=1700000000, bytes_accessed=10000000, transcendentals=0),
    )(
        mu_atom,
        mu_target,
        mu_sizes,
        nu_sizes,
        screen.reshape(screen.shape[0]),
        b_tensor.reshape(NP, NB, BS, BS),
        virt_green.reshape(NB, BS, SIG),
        occ_green,
    )
    return out.reshape(SIG // NROW, 1, 128)


def solution(mesh):
    placed = (
        P(None, "row", "dep"),
        P("dep", "col"),
        P("row", None),
        P(),
        P(),
        P(),
        P("dep"),
        P(None, "dep"),
    )
    return jax.shard_map(
        body, mesh=mesh, in_specs=placed, out_specs=P("row", "dep", "col"), check_vma=False
    )
```

time: 63.1 us -> 63.2 us (level)
  no operation moved by 1% of the time
where the time goes in v2:
time: 63.2 us; the launch traced here: 63 us
  Pallas kernels  61 us (97%)
  local copies, waits for them, and re-layouts  1.32 us (2%)
  between operations  0.66 us (1%)
    pallas_call x1, Pallas kernels, body(): pl.pallas_call(kernel, name='contract', out_shape=jax.ShapeDtypeStruct((N...  61 us
    unnamed x1, local copies, waits for them, and re-layouts  1.32 us

profile of v2, /device:TPU:8, one launch (start us, length us, event | category | flops | bytes accessed | tf_op | source)
XLA Modules:
  0.0 63.0 jit_solution(13302654486190934172)
XLA Ops:
  0.7 61.0 %contract.1 = f32[4,8,128]{2,1,0:T(8,128)} custom-call(s32[96]{0:T(128)} %atom_ref.1, s32[96]{0:T(128)} %target_ref.1, s32[96]{0:T(128)} %size_ref.1, s32[1]{0:T(128)S(6)} %copy.11.nu_ref, s32[96]{0:T(128)} %bitcast.9, bf16[12,6,256,256]{3,2,1,0:T(8,128)(2,1)} %bitcast.6, bf16[6,256,512]{2,1,0:T(8,128)(2,1)} %bitcast.7, bf16[256,128]{1,0:T(8,128)(2,1)} %occ_ref.1), custom_call_target="tpu_custom_call" | custom-call | flops 1700000000 | bytes 10000000 | tf_op jit(solution)/shard_map/contract/pallas_call | solution.py:255
  61.7 1.3 %copy.12 = f32[32,1,128]{2,1,0:T(1,128)} copy(f32[32,1,128]{2,1,0:T(1,128)} %bitcast.8) | data formatting | bytes 32768

commit v3 on v1

v3 whole, which is shorter than its diff:
```python
import jax
import jax.numpy as jnp
from jax import lax
from jax.experimental import pallas as pl
from jax.experimental.pallas import tpu as pltpu
from jax.sharding import PartitionSpec as P

MESH = pl.DeviceIdType.MESH
BF16 = jnp.bfloat16
F32 = jnp.float32

BS = 256
NB = 6
KEPT = 208
SHARE = 64
TAIL = KEPT - 3 * SHARE
NROW, NCOL, NDEP = 16, 4, 12
NY = NROW // 2
NP = 12
SIG = 512
LAG = 2
GROUPS = 6
P_GROUP = NP // GROUPS
ROWS_GROUP = P_GROUP * 8


def wrap(value, size):
    return jnp.where(value >= size, value - size, value)


def arrived(ref, sem):
    pltpu.make_async_copy(ref, ref, sem).wait()


def kernel(
    atom_ref,
    target_ref,
    size_ref,
    nu_ref,
    screen_ref,
    b_ref,
    virt_ref,
    occ_ref,
    out_ref,
    b_buf,
    virt_buf,
    occ_buf,
    occ_kept,
    picked,
    green_out,
    green_in,
    green_all,
    y_buf,
    y_pair,
    y_out,
    y_in,
    w_out,
    w_in,
    b_sem,
    local_sem,
    green_send,
    green_recv,
    share_send,
    share_recv,
    occ_send,
    occ_recv,
    pair_send,
    pair_recv,
    y_send,
    y_recv,
    w_send,
    w_recv,
):
    row, col, dep = lax.axis_index("row"), lax.axis_index("col"), lax.axis_index("dep")
    core = lax.rem(row, 2)
    y = lax.div(row, 2)
    other = 1 - core
    share = lax.rem(dep, 3)
    here = pl.ds(pl.multiple_of(share * SHARE, SHARE), SHARE)
    tail = pl.ds(3 * SHARE, TAIL)

    rows_of = [wrap(row + o, NROW) for o in range(NROW)]
    ys_of = [wrap(y + o, NY) for o in range(NY)]
    cols_of = [wrap(col + o, NCOL) for o in range(NCOL)]
    deps_of = [wrap(dep + o, NDEP) for o in range(NDEP)]
    virt_copies = [
        pltpu.make_async_copy(virt_ref.at[:, here, :], virt_buf.at[:, pl.ds(0, SHARE), :], local_sem.at[0]),
        pltpu.make_async_copy(virt_ref.at[:, tail, :], virt_buf.at[:, pl.ds(SHARE, TAIL), :], local_sem.at[1]),
    ]
    for copy in virt_copies:
        copy.start()
    barrier = pltpu.get_barrier_semaphore()
    for o in (6, 5, 7, 4, 8, 3, 9, 2, 10, 1, 11):
        pl.semaphore_signal(barrier, inc=1, device_id=(row, col, deps_of[o]), device_id_type=MESH)
    for o in range(1, NROW):
        pl.semaphore_signal(barrier, inc=1, device_id=(rows_of[o], col, dep), device_id_type=MESH)
    for o in range(1, NCOL):
        pl.semaphore_signal(barrier, inc=1, device_id=(row, cols_of[o], dep), device_id_type=MESH)

    first = row * NB
    wanted = []
    for o in range(NROW):
        found = jnp.int32(0)
        for j in range(NB):
            t = target_ref[atom_ref[rows_of[o] * NB + j]] - first
            found += jnp.where((t >= 0) & (t < NB), t, 0)
        wanted.append(found)

    q = lax.broadcasted_iota(jnp.int32, (1, 128), 1)
    column = (2 * ((q >> 3) & 7) + (q >> 6)) * 32 + col * 8 + (q & 7)
    choose = jnp.where(lax.broadcasted_iota(jnp.int32, (SIG, 128), 0) == column, 1.0, 0.0).astype(BF16)
    for copy in virt_copies:
        copy.wait()
    picked[...] = (
        jnp.dot(virt_buf[...].reshape(NB * (SHARE + TAIL), SIG), choose, preferred_element_type=F32)
        .astype(BF16)
        .reshape(NB, SHARE + TAIL, 128)
    )
    for o in range(NROW):
        if o == 0:
            green_in[row] = picked[wanted[o]]
        else:
            green_out[o] = picked[wanted[o]]

    pl.semaphore_wait(barrier, NDEP + NROW + NCOL - 3)
    sent = []

    for o in (8, 9, 7, 10, 6, 11, 5, 12, 4, 13, 3, 14, 2, 15, 1):
        copy = pltpu.make_async_remote_copy(
            green_out.at[o], green_in.at[row], green_send.at[0], green_recv.at[0],
            device_id=(rows_of[o], col, dep), device_id_type=MESH,
        )
        copy.start()
    mine = pl.multiple_of(col * 128, 128)
    occ_copy = pltpu.make_async_copy(occ_ref, occ_buf.at[:, pl.ds(mine, 128)], local_sem.at[2])
    occ_copy.start()
    b_copies = [
        pltpu.make_async_copy(b_ref.at[p, :, pl.ds(0, KEPT), :], b_buf.at[p], b_sem.at[p]) for p in range(NP)
    ]

    for copy in b_copies:
        copy.start()
    occ_copy.wait()
    for o in range(1, NCOL):
        copy = pltpu.make_async_remote_copy(
            occ_buf.at[:, pl.ds(mine, 128)], occ_buf.at[:, pl.ds(mine, 128)], occ_send.at[o], occ_recv.at[col],
            device_id=(row, cols_of[o], dep), device_id_type=MESH,
        )
        copy.start()
        sent.append(copy)

    arrived(green_out.at[pl.ds(1, NROW - 1)], green_recv.at[0])

    for j in range(NB):
        source = target_ref[atom_ref[row * NB + j]] // NB
        block = green_in[source]
        green_all[j, here, :] = block[:SHARE]
        green_all[j, tail, :] = block[SHARE:]
    for o in (1, NDEP - 1):
        copy = pltpu.make_async_remote_copy(
            green_all.at[:, here, :], green_all.at[:, here, :], share_send.at[o // 11], share_recv.at[o // 11],
            device_id=(row, col, deps_of[o]), device_id_type=MESH,
        )
        copy.start()
        sent.append(copy)
    for o in range(1, NCOL):
        piece = occ_buf.at[:, pl.ds(pl.multiple_of(cols_of[o] * 128, 128), 128)]
        arrived(piece, occ_recv.at[cols_of[o]])
    inside = lax.broadcasted_iota(jnp.int32, (BS, SIG), 0) < nu_ref[0]
    occ_kept[...] = jnp.where(inside, occ_buf[...].astype(F32), 0.0).astype(BF16)
    before = pl.ds(pl.multiple_of(lax.rem(share + 2, 3) * SHARE, SHARE), SHARE)
    after = pl.ds(pl.multiple_of(lax.rem(share + 1, 3) * SHARE, SHARE), SHARE)
    arrived(green_all.at[:, before, :], share_recv.at[0])
    arrived(green_all.at[:, after, :], share_recv.at[1])

    parts = []
    for j in range(NB):
        atom = atom_ref[row * NB + j]
        kept = size_ref[atom] * screen_ref[atom]
        inside = lax.broadcasted_iota(jnp.int32, (KEPT, 128), 0) < kept
        parts.append(jnp.where(inside, green_all[j].astype(F32), 0.0).astype(BF16))
    rows_first = jnp.concatenate(parts, axis=0)
    green = rows_first.T

    pair_copies = []

    def contract_first(g):
        for h in range(P_GROUP // 2):
            halves = []
            for k in range(2):
                p = g * P_GROUP + 2 * h + k
                b_copies[p].wait()
                block = b_buf[p].reshape(NB * KEPT, BS)
                halves.append(jnp.dot(green, block, preferred_element_type=F32).reshape(2, NY, 8, BS))
            y_buf[g, :, :, pl.ds(h * 16, 16), :] = jnp.concatenate(halves, axis=2).astype(BF16)
        copy = pltpu.make_async_remote_copy(
            y_buf.at[g, other], y_pair.at[g], pair_send.at[g], pair_recv.at[g],
            device_id=(row + 1 - 2 * core, col, dep), device_id_type=MESH,
        )
        copy.start()
        pair_copies.append(copy)
        sent.append(copy)

    def send_over_y(g):
        pair_copies[g].wait_recv()
        y_out[g] = (y_buf[g, core].astype(F32) + y_pair[g].astype(F32)).astype(BF16)
        for o in (4, 5, 3, 6, 2, 7, 1):
            copy = pltpu.make_async_remote_copy(
                y_out.at[g, ys_of[o]], y_in.at[g, y], y_send.at[0], y_recv.at[g],
                device_id=(2 * ys_of[o] + core, col, dep), device_id_type=MESH,
            )
            copy.start()
        y_in[g, y] = y_out[g, y]

    for g in range(GROUPS):
        contract_first(g)
        if g >= LAG:
            send_over_y(g - LAG)
    for g in range(GROUPS - LAG, GROUPS):
        send_over_y(g)

    for g in range(GROUPS):
        arrived(y_out.at[g, pl.ds(1, NY - 1)], y_recv.at[g])
        total = y_in[g, 0].astype(F32)
        for k in range(1, NY):
            total += y_in[g, k].astype(F32)
        w = jnp.dot(total.astype(BF16), occ_kept[...], preferred_element_type=F32)
        for k in range(P_GROUP):
            p = g * P_GROUP + k
            for c in range(NCOL):
                w_out[p * NCOL + c] = w[k * 8 : (k + 1) * 8, c * 128 : (c + 1) * 128]
            for o in (2, 1, 3, 0):
                c = cols_of[o]

                def send():
                    pltpu.make_async_remote_copy(
                        w_out.at[p * NCOL + c], w_in.at[dep * NCOL + col], w_send.at[0], w_recv.at[0],
                        device_id=(row, c, p), device_id_type=MESH,
                    ).start()

                if o == 0:
                    pl.when(dep != p)(send)
                else:
                    send()

    w_in[dep * NCOL + col] = w_out[dep * NCOL + col]
    others = pl.ds(1, NDEP * NCOL - 1)
    arrived(w_in.at[others], w_recv.at[0])
    for c in range(NCOL):
        result = w_in[c]
        for k in range(1, NDEP):
            result += w_in[k * NCOL + c]
        out_ref[c] = result
    arrived(w_out.at[others], w_send.at[0])
    arrived(green_out.at[pl.ds(1, NROW - 1)], green_send.at[0])
    arrived(y_out.at[:, pl.ds(1, NY - 1)], y_send.at[0])
    for copy in sent:
        copy.wait_send()


def body(b_tensor, occ_green, virt_green, mu_atom, mu_target, mu_sizes, nu_sizes, screen):
    smem = pl.BlockSpec(memory_space=pltpu.SMEM)
    hbm = pl.BlockSpec(memory_space=pl.ANY)
    dma = pltpu.SemaphoreType.DMA
    out = pl.pallas_call(
        kernel,
        name="contract",
        out_shape=jax.ShapeDtypeStruct((NCOL, 8, 128), F32),
        in_specs=[smem] * 5 + [hbm] * 3,
        out_specs=pl.BlockSpec(memory_space=pltpu.VMEM),
        scratch_shapes=[
            pltpu.VMEM((NP, NB, KEPT, BS), BF16),
            pltpu.VMEM((NB, SHARE + TAIL, SIG), BF16),
            pltpu.VMEM((BS, SIG), BF16),
            pltpu.VMEM((BS, SIG), BF16),
            pltpu.VMEM((NB, SHARE + TAIL, 128), BF16),
            pltpu.VMEM((NROW, SHARE + TAIL, 128), BF16),
            pltpu.VMEM((NROW, SHARE + TAIL, 128), BF16),
            pltpu.VMEM((NB, KEPT, 128), BF16),
            pltpu.VMEM((GROUPS, 2, NY, ROWS_GROUP, BS), BF16),
            pltpu.VMEM((GROUPS, NY, ROWS_GROUP, BS), BF16),
            pltpu.VMEM((GROUPS, NY, ROWS_GROUP, BS), BF16),
            pltpu.VMEM((GROUPS, NY, ROWS_GROUP, BS), BF16),
            pltpu.VMEM((NP * NCOL, 8, 128), F32),
            pltpu.VMEM((NDEP * NCOL, 8, 128), F32),
            dma((NP,)),
            dma((3,)),
            dma((1,)),
            dma((1,)),
            dma((2,)),
            dma((2,)),
            dma((NCOL,)),
            dma((NCOL,)),
            dma((GROUPS,)),
            dma((GROUPS,)),
            dma((1,)),
            dma((GROUPS,)),
            dma((1,)),
            dma((1,)),
        ],
        compiler_params=pltpu.CompilerParams(
            collective_id=0, has_side_effects=True, vmem_limit_bytes=56 * 2**20
        ),
        cost_estimate=pl.CostEstimate(flops=1700000000, bytes_accessed=10000000, transcendentals=0),
    )(
        mu_atom,
        mu_target,
        mu_sizes,
        nu_sizes,
        screen.reshape(screen.shape[0]),
        b_tensor.reshape(NP, NB, BS, BS),
        virt_green.reshape(NB, BS, SIG),
        occ_green,
    )
    return out.reshape(SIG // NROW, 1, 128)


def solution(mesh):
    placed = (
        P(None, "row", "dep"),
        P("dep", "col"),
        P("row", None),
        P(),
        P(),
        P(),
        P("dep"),
        P(None, "dep"),
    )
    return jax.shard_map(
        body, mesh=mesh, in_specs=placed, out_specs=P("row", "dep", "col"), check_vma=False
    )
```

time: 63.1 us -> 52.8 us (0.84)
  the two profiles are of different devices: /device:TPU:8 before, /device:TPU:1 now
where the time goes in v3:
time: 52.8 us; the launch traced here: 52.4 us
  Pallas kernels  50.4 us (95%)
  local copies, waits for them, and re-layouts  1.32 us (2%)
  between operations  0.66 us (1%)
    pallas_call x1, Pallas kernels, body(): pl.pallas_call(kernel, name='contract', out_shape=jax.ShapeDtypeStruct((N...  50.4 us
    unnamed x1, local copies, waits for them, and re-layouts  1.32 us

profile of v3, /device:TPU:1, one launch (start us, length us, event | category | flops | bytes accessed | tf_op | source)
XLA Modules:
  0.0 52.4 jit_solution(2892073754722674858)
XLA Ops:
  0.7 50.4 %contract.1 = f32[4,8,128]{2,1,0:T(8,128)} custom-call(s32[96]{0:T(128)} %atom_ref.1, s32[96]{0:T(128)} %target_ref.1, s32[96]{0:T(128)} %size_ref.1, s32[1]{0:T(128)S(6)} %copy.11.nu_ref, s32[96]{0:T(128)} %bitcast.9, bf16[12,6,256,256]{3,2,1,0:T(8,128)(2,1)} %bitcast.6, bf16[6,256,512]{2,1,0:T(8,128)(2,1)} %bitcast.7, bf16[256,128]{1,0:T(8,128)(2,1)} %occ_ref.1), custom_call_target="tpu_custom_call" | custom-call | flops 1700000000 | bytes 10000000 | tf_op jit(solution)/shard_map/contract/pallas_call | solution.py:265
  51.1 1.3 %copy.12 = f32[32,1,128]{2,1,0:T(1,128)} copy(f32[32,1,128]{2,1,0:T(1,128)} %bitcast.8) | data formatting | bytes 32768

commit v4 on v3

v4 whole, which is shorter than its diff:
```python
import jax
import jax.numpy as jnp
from jax import lax
from jax.experimental import pallas as pl
from jax.experimental.pallas import tpu as pltpu
from jax.sharding import PartitionSpec as P

MESH = pl.DeviceIdType.MESH
BF16 = jnp.bfloat16
F32 = jnp.float32

BS = 256
NB = 6
KEPT = 208
SHARE = 64
TAIL = KEPT - 3 * SHARE
NROW, NCOL, NDEP = 16, 4, 12
NY = NROW // 2
NP = 12
SIG = 512
PAIRS = NP // 4
FAR_FIRST = (8, 9, 7, 10, 6, 11, 5, 12, 4, 13, 3, 14, 2, 15, 1)


def wrap(value, size):
    return jnp.where(value >= size, value - size, value)


def arrived(ref, sem):
    pltpu.make_async_copy(ref, ref, sem).wait()


def kernel(
    atom_ref,
    target_ref,
    size_ref,
    nu_ref,
    screen_ref,
    b_ref,
    virt_ref,
    occ_ref,
    out_ref,
    b_buf,
    virt_buf,
    occ_buf,
    occ_kept,
    picked,
    green_out,
    green_in,
    green_all,
    green_ref,
    y_buf,
    y_pair,
    y_out,
    y_in,
    w_out,
    w_in,
    b_sem,
    local_sem,
    green_send,
    green_recv,
    share_send,
    share_recv,
    occ_send,
    occ_recv,
    pair_send,
    pair_recv,
    y_send,
    y_recv,
    w_send,
    w_recv,
):
    row, col, dep = lax.axis_index("row"), lax.axis_index("col"), lax.axis_index("dep")
    core = lax.rem(row, 2)
    y = lax.div(row, 2)
    other = 1 - core
    parity = lax.div(col, 2)
    share = lax.rem(dep, 3)
    here = pl.ds(pl.multiple_of(share * SHARE, SHARE), SHARE)
    tail = pl.ds(3 * SHARE, TAIL)

    rows_of = [wrap(row + o, NROW) for o in range(NROW)]
    ys_of = [wrap(y + o, NY) for o in range(NY)]
    cols_of = [wrap(col + o, NCOL) for o in range(NCOL)]
    deps_of = [wrap(dep + o, NDEP) for o in range(NDEP)]
    virt_copies = [
        pltpu.make_async_copy(virt_ref.at[:, here, :], virt_buf.at[:, pl.ds(0, SHARE), :], local_sem.at[0]),
        pltpu.make_async_copy(virt_ref.at[:, tail, :], virt_buf.at[:, pl.ds(SHARE, TAIL), :], local_sem.at[1]),
    ]
    for copy in virt_copies:
        copy.start()
    barrier = pltpu.get_barrier_semaphore()
    for o in (6, 5, 7, 4, 8, 3, 9, 2, 10, 1, 11):
        pl.semaphore_signal(barrier, inc=1, device_id=(row, col, deps_of[o]), device_id_type=MESH)
    for o in FAR_FIRST:
        pl.semaphore_signal(barrier, inc=1, device_id=(rows_of[o], col, dep), device_id_type=MESH)
    for o in range(1, NCOL):
        pl.semaphore_signal(barrier, inc=1, device_id=(row, cols_of[o], dep), device_id_type=MESH)

    q = lax.broadcasted_iota(jnp.int32, (1, 128), 1)
    column = (2 * (q >> 4) + parity) * 32 + lax.rem(col, 2) * 16 + (q & 15)
    choose = jnp.where(lax.broadcasted_iota(jnp.int32, (SIG, 128), 0) == column, 1.0, 0.0).astype(BF16)
    for copy in virt_copies:
        copy.wait()
    picked[...] = (
        jnp.dot(virt_buf[...].reshape(NB * (SHARE + TAIL), SIG), choose, preferred_element_type=F32)
        .astype(BF16)
        .reshape(NB, SHARE + TAIL, 128)
    )

    first = row * NB

    @pl.loop(0, NROW)
    def _(r):
        found = jnp.int32(0)
        for j in range(NB):
            t = target_ref[atom_ref[r * NB + j]] - first
            found += jnp.where((t >= 0) & (t < NB), t, 0)
        green_out[r] = picked[found]

    pl.semaphore_wait(barrier, NDEP + NROW + NCOL - 3)
    sent = []

    @pl.loop(0, NROW - 1)
    def _(i):
        o = jnp.where(lax.rem(i, 2) == 1, NY + lax.div(i + 1, 2), NY - lax.div(i, 2))
        to = wrap(row + o, NROW)
        pltpu.make_async_remote_copy(
            green_out.at[to], green_in.at[row], green_send.at[0], green_recv.at[0],
            device_id=(to, col, dep), device_id_type=MESH,
        ).start()

    green_in[row] = green_out[row]
    mine = pl.multiple_of(col * 128, 128)
    occ_copy = pltpu.make_async_copy(occ_ref, occ_buf.at[:, pl.ds(mine, 128)], local_sem.at[2])
    occ_copy.start()

    @pl.loop(0, NP)
    def _(p):
        pltpu.make_async_copy(b_ref.at[p, :, pl.ds(0, KEPT), :], b_buf.at[p], b_sem.at[p]).start()

    arrived(green_out.at[pl.ds(1, NROW - 1)], green_recv.at[0])

    for j in range(NB):
        source = target_ref[atom_ref[row * NB + j]] // NB
        block = green_in[source]
        green_all[j, here, :] = block[:SHARE]
        green_all[j, tail, :] = block[SHARE:]
    for o in (1, NDEP - 1):
        copy = pltpu.make_async_remote_copy(
            green_all.at[:, here, :], green_all.at[:, here, :], share_send.at[o // 11], share_recv.at[o // 11],
            device_id=(row, col, deps_of[o]), device_id_type=MESH,
        )
        copy.start()
        sent.append(copy)
    occ_copy.wait()
    for o in range(1, NCOL):
        copy = pltpu.make_async_remote_copy(
            occ_buf.at[:, pl.ds(mine, 128)], occ_buf.at[:, pl.ds(mine, 128)], occ_send.at[o], occ_recv.at[col],
            device_id=(row, cols_of[o], dep), device_id_type=MESH,
        )
        copy.start()
        sent.append(copy)
    before = pl.ds(pl.multiple_of(lax.rem(share + 2, 3) * SHARE, SHARE), SHARE)
    after = pl.ds(pl.multiple_of(lax.rem(share + 1, 3) * SHARE, SHARE), SHARE)
    arrived(green_all.at[:, before, :], share_recv.at[0])
    arrived(green_all.at[:, after, :], share_recv.at[1])

    parts = []
    for j in range(NB):
        atom = atom_ref[row * NB + j]
        kept = size_ref[atom] * screen_ref[atom]
        inside = lax.broadcasted_iota(jnp.int32, (KEPT, 128), 0) < kept
        parts.append(jnp.where(inside, green_all[j].astype(F32), 0.0).astype(BF16))
    rows_first = jnp.concatenate(parts, axis=0)
    green_ref[...] = rows_first.T


    def pair_copy(m):
        return pltpu.make_async_remote_copy(
            y_buf.at[2 * m + other], y_pair.at[m], pair_send.at[m], pair_recv.at[m],
            device_id=(row + 1 - 2 * core, col, dep), device_id_type=MESH,
        )

    def contract_first(m, owner):
        @pl.loop(0, 2)
        def _(k):
            p = 4 * m + 2 * owner + k
            arrived(b_buf.at[p], b_sem.at[p])
            block = b_buf[p].reshape(NB * KEPT, BS)
            product = jnp.dot(green_ref[...], block, preferred_element_type=F32).astype(BF16).reshape(NY, 16, BS)
            y_buf[2 * m + owner, :, pl.ds(pl.multiple_of(k * 16, 16), 16), :] = product

    @pl.loop(0, PAIRS)
    def _(m):
        @pl.loop(0, 2)
        def _(t):
            contract_first(m, jnp.where(t == 0, other, core))
            pl.when(t == 0)(lambda: pair_copy(m).start())
        pair_copy(m).wait_recv()
        y_out[m] = (y_buf[2 * m + core].astype(F32) + y_pair[m].astype(F32)).astype(BF16)
        @pl.loop(0, NY - 1)
        def _(i):
            half = NY // 2
            o = jnp.where(lax.rem(i, 2) == 1, half + lax.div(i + 1, 2), half - lax.div(i, 2))
            to = wrap(y + o, NY)
            pltpu.make_async_remote_copy(
                y_out.at[m, to], y_in.at[m, y], y_send.at[0], y_recv.at[m],
                device_id=(2 * to + core, col, dep), device_id_type=MESH,
            ).start()

        y_in[m, y] = y_out[m, y]

    for o in range(1, NCOL):
        piece = occ_buf.at[:, pl.ds(pl.multiple_of(cols_of[o] * 128, 128), 128)]
        arrived(piece, occ_recv.at[cols_of[o]])
    inside = lax.broadcasted_iota(jnp.int32, (BS, SIG), 0) < nu_ref[0]
    occ_kept[...] = jnp.where(inside, occ_buf[...].astype(F32), 0.0).astype(BF16)

    own = (core == parity) & (lax.rem(lax.div(dep, 2), 2) == core)
    @pl.loop(0, PAIRS)
    def _(m):
        arrived(y_out.at[m, pl.ds(1, NY - 1)], y_recv.at[m])
        total = y_in[m, 0].astype(F32)
        for k in range(1, NY):
            total += y_in[m, k].astype(F32)
        w = jnp.dot(total.astype(BF16), occ_kept[...], preferred_element_type=F32).astype(BF16)
        for k in range(2):
            for c in range(NCOL):
                w_out[(2 * m + k) * NCOL + c] = w[k * 16 : (k + 1) * 16, c * 128 : (c + 1) * 128]
        @pl.loop(0, 2 * NCOL)
        def _(i):
            p = 4 * m + 2 * core + lax.div(i, NCOL)
            c = lax.rem(i, NCOL)
            slot = 2 * m * NCOL + i
            same = own & (dep == p) & (col == c)

            @pl.when(jnp.logical_not(same))
            def _():
                pltpu.make_async_remote_copy(
                    w_out.at[slot], w_in.at[dep * 2 + lax.rem(col, 2)], w_send.at[0], w_recv.at[0],
                    device_id=(2 * y + parity, c, p), device_id_type=MESH,
                ).start()

            @pl.when(same)
            def _():
                w_in[dep * 2 + lax.rem(col, 2)] = w_out[slot]

    @pl.when(own)
    def _():
        arrived(w_in.at[pl.ds(0, 2 * NDEP - 1)], w_recv.at[0])

    @pl.when(jnp.logical_not(own))
    def _():
        arrived(w_in, w_recv.at[0])

    for c in range(2):
        result = w_in[c].astype(F32)
        for k in range(1, NDEP):
            result += w_in[2 * k + c].astype(F32)
        out_ref[c] = result

    @pl.when(own)
    def _():
        arrived(w_out.at[pl.ds(0, 2 * NDEP - 1)], w_send.at[0])

    @pl.when(jnp.logical_not(own))
    def _():
        arrived(w_out, w_send.at[0])
    arrived(green_out.at[pl.ds(1, NROW - 1)], green_send.at[0])
    arrived(y_out.at[:, pl.ds(1, NY - 1)], y_send.at[0])
    for m in range(PAIRS):
        pair_copy(m).wait_send()
    for copy in sent:
        copy.wait_send()


def body(b_tensor, occ_green, virt_green, mu_atom, mu_target, mu_sizes, nu_sizes, screen):
    smem = pl.BlockSpec(memory_space=pltpu.SMEM)
    hbm = pl.BlockSpec(memory_space=pl.ANY)
    dma = pltpu.SemaphoreType.DMA
    out = pl.pallas_call(
        kernel,
        name="contract",
        out_shape=jax.ShapeDtypeStruct((2, 16, 128), F32),
        in_specs=[smem] * 5 + [hbm] * 3,
        out_specs=pl.BlockSpec(memory_space=pltpu.VMEM),
        scratch_shapes=[
            pltpu.VMEM((NP, NB, KEPT, BS), BF16),
            pltpu.VMEM((NB, SHARE + TAIL, SIG), BF16),
            pltpu.VMEM((BS, SIG), BF16),
            pltpu.VMEM((BS, SIG), BF16),
            pltpu.VMEM((NB, SHARE + TAIL, 128), BF16),
            pltpu.VMEM((NROW, SHARE + TAIL, 128), BF16),
            pltpu.VMEM((NROW, SHARE + TAIL, 128), BF16),
            pltpu.VMEM((NB, KEPT, 128), BF16),
            pltpu.VMEM((128, NB * KEPT), BF16),
            pltpu.VMEM((2 * PAIRS, NY, 32, BS), BF16),
            pltpu.VMEM((PAIRS, NY, 32, BS), BF16),
            pltpu.VMEM((PAIRS, NY, 32, BS), BF16),
            pltpu.VMEM((PAIRS, NY, 32, BS), BF16),
            pltpu.VMEM((2 * PAIRS * NCOL, 16, 128), BF16),
            pltpu.VMEM((2 * NDEP, 16, 128), BF16),
            dma((NP,)),
            dma((3,)),
            dma((1,)),
            dma((1,)),
            dma((2,)),
            dma((2,)),
            dma((NCOL,)),
            dma((NCOL,)),
            dma((PAIRS,)),
            dma((PAIRS,)),
            dma((1,)),
            dma((PAIRS,)),
            dma((1,)),
            dma((1,)),
        ],
        compiler_params=pltpu.CompilerParams(
            collective_id=0, has_side_effects=True, vmem_limit_bytes=56 * 2**20
        ),
        cost_estimate=pl.CostEstimate(flops=1700000000, bytes_accessed=10000000, transcendentals=0),
    )(
        mu_atom,
        mu_target,
        mu_sizes,
        nu_sizes,
        screen.reshape(screen.shape[0]),
        b_tensor.reshape(NP, NB, BS, BS),
        virt_green.reshape(NB, BS, SIG),
        occ_green,
    )
    return out.reshape(SIG // NROW, 1, 128)


def solution(mesh):
    placed = (
        P(None, "row", "dep"),
        P("dep", "col"),
        P("row", None),
        P(),
        P(),
        P(),
        P("dep"),
        P(None, "dep"),
    )
    return jax.shard_map(
        body, mesh=mesh, in_specs=placed, out_specs=P("row", "dep", "col"), check_vma=False
    )
```

time: 52.8 us -> 51.1 us (0.968)
  Pallas kernels: 50.4 us -> 48.8 us
    pallas_call x1, Pallas kernels: 50.4 us -> 48.8 us  [body(): pl.pallas_call(kernel, name='contract', out_shape=jax.ShapeDtypeStruct((2...]
where the time goes in v4:
time: 51.1 us; the launch traced here: 50.8 us
  Pallas kernels  48.8 us (95%)
  local copies, waits for them, and re-layouts  1.32 us (3%)
  between operations  0.66 us (1%)
    pallas_call x1, Pallas kernels, body(): pl.pallas_call(kernel, name='contract', out_shape=jax.ShapeDtypeStruct((2...  48.8 us
    unnamed x1, local copies, waits for them, and re-layouts  1.32 us

profile of v4, /device:TPU:1, one launch (start us, length us, event | category | flops | bytes accessed | tf_op | source)
XLA Modules:
  0.0 50.8 jit_solution(1699510077819617599)
XLA Ops:
  0.7 48.8 %contract.1 = f32[2,16,128]{2,1,0:T(8,128)} custom-call(s32[96]{0:T(128)} %atom_ref.1, s32[96]{0:T(128)} %target_ref.1, s32[96]{0:T(128)} %size_ref.1, s32[1]{0:T(128)S(6)} %copy.11.nu_ref, s32[96]{0:T(128)} %bitcast.9, bf16[12,6,256,256]{3,2,1,0:T(8,128)(2,1)} %bitcast.6, bf16[6,256,512]{2,1,0:T(8,128)(2,1)} %bitcast.7, bf16[256,128]{1,0:T(8,128)(2,1)} %occ_ref.1), custom_call_target="tpu_custom_call" | custom-call | flops 1700000000 | bytes 10000000 | tf_op jit(solution)/shard_map/contract/pallas_call | solution.py:282
  49.5 1.3 %copy.12 = f32[32,1,128]{2,1,0:T(1,128)} copy(f32[32,1,128]{2,1,0:T(1,128)} %bitcast.8) | data formatting | bytes 32768

commit v5 on v4

--- a/solution.py
+++ b/solution.py
@@ -18,7 +18,8 @@
 NY = NROW // 2
 NP = 12
 SIG = 512
-PAIRS = NP // 4
+STEPS = NP // 2
+Y_ORDER = (0, 1, 2, 7, 3, 6, 5, 4)
 FAR_FIRST = (8, 9, 7, 10, 6, 11, 5, 12, 4, 13, 3, 14, 2, 15, 1)
 
 
@@ -183,31 +184,33 @@
         )
 
     def contract_first(m, owner):
-        @pl.loop(0, 2)
-        def _(k):
-            p = 4 * m + 2 * owner + k
-            arrived(b_buf.at[p], b_sem.at[p])
-            block = b_buf[p].reshape(NB * KEPT, BS)
-            product = jnp.dot(green_ref[...], block, preferred_element_type=F32).astype(BF16).reshape(NY, 16, BS)
-            y_buf[2 * m + owner, :, pl.ds(pl.multiple_of(k * 16, 16), 16), :] = product
-
-    @pl.loop(0, PAIRS)
+        p = 2 * m + owner
+        arrived(b_buf.at[p], b_sem.at[p])
+        block = b_buf[p].reshape(NB * KEPT, BS)
+        product = jnp.dot(green_ref[...], block, preferred_element_type=F32).astype(BF16).reshape(NY, 16, BS)
+        y_buf[p] = product
+
+    contract_first(0, other)
+    pair_copy(0).start()
+
+    @pl.loop(0, STEPS)
     def _(m):
-        @pl.loop(0, 2)
-        def _(t):
-            contract_first(m, jnp.where(t == 0, other, core))
-            pl.when(t == 0)(lambda: pair_copy(m).start())
+        contract_first(m, core)
+
+        @pl.when(m < STEPS - 1)
+        def _():
+            contract_first(m + 1, other)
+            pair_copy(m + 1).start()
+
         pair_copy(m).wait_recv()
         y_out[m] = (y_buf[2 * m + core].astype(F32) + y_pair[m].astype(F32)).astype(BF16)
-        @pl.loop(0, NY - 1)
-        def _(i):
-            half = NY // 2
-            o = jnp.where(lax.rem(i, 2) == 1, half + lax.div(i + 1, 2), half - lax.div(i, 2))
-            to = wrap(y + o, NY)
-            pltpu.make_async_remote_copy(
-                y_out.at[m, to], y_in.at[m, y], y_send.at[0], y_recv.at[m],
-                device_id=(2 * to + core, col, dep), device_id_type=MESH,
-            ).start()
+        for to in Y_ORDER:
+            @pl.when(to != y)
+            def _():
+                pltpu.make_async_remote_copy(
+                    y_out.at[m, to], y_in.at[m, y], y_send.at[0], y_recv.at[m],
+                    device_id=(2 * to + core, col, dep), device_id_type=MESH,
+                ).start()
 
         y_in[m, y] = y_out[m, y]
 
@@ -217,29 +220,27 @@
     inside = lax.broadcasted_iota(jnp.int32, (BS, SIG), 0) < nu_ref[0]
     occ_kept[...] = jnp.where(inside, occ_buf[...].astype(F32), 0.0).astype(BF16)
 
-    own = (core == parity) & (lax.rem(lax.div(dep, 2), 2) == core)
-    @pl.loop(0, PAIRS)
+    own = (core == parity) & (lax.rem(dep, 2) == core)
+    @pl.loop(0, STEPS)
     def _(m):
         arrived(y_out.at[m, pl.ds(1, NY - 1)], y_recv.at[m])
         total = y_in[m, 0].astype(F32)
         for k in range(1, NY):
             total += y_in[m, k].astype(F32)
         w = jnp.dot(total.astype(BF16), occ_kept[...], preferred_element_type=F32).astype(BF16)
-        for k in range(2):
-            for c in range(NCOL):
-                w_out[(2 * m + k) * NCOL + c] = w[k * 16 : (k + 1) * 16, c * 128 : (c + 1) * 128]
-        @pl.loop(0, 2 * NCOL)
+        for c in range(NCOL):
+            w_out[m * NCOL + c] = w[:, c * 128 : (c + 1) * 128]
+        @pl.loop(0, NCOL)
         def _(i):
-            p = 4 * m + 2 * core + lax.div(i, NCOL)
-            c = lax.rem(i, NCOL)
-            slot = 2 * m * NCOL + i
-            same = own & (dep == p) & (col == c)
+            p = 2 * m + core
+            slot = m * NCOL + i
+            same = own & (dep == p) & (col == i)
 
             @pl.when(jnp.logical_not(same))
             def _():
                 pltpu.make_async_remote_copy(
                     w_out.at[slot], w_in.at[dep * 2 + lax.rem(col, 2)], w_send.at[0], w_recv.at[0],
-                    device_id=(2 * y + parity, c, p), device_id_type=MESH,
+                    device_id=(2 * y + parity, i, p), device_id_type=MESH,
                 ).start()
 
             @pl.when(same)
@@ -269,7 +270,7 @@
         arrived(w_out, w_send.at[0])
     arrived(green_out.at[pl.ds(1, NROW - 1)], green_send.at[0])
     arrived(y_out.at[:, pl.ds(1, NY - 1)], y_send.at[0])
-    for m in range(PAIRS):
+    for m in range(STEPS):
         pair_copy(m).wait_send()
     for copy in sent:
         copy.wait_send()
@@ -295,11 +296,11 @@
             pltpu.VMEM((NROW, SHARE + TAIL, 128), BF16),
             pltpu.VMEM((NB, KEPT, 128), BF16),
             pltpu.VMEM((128, NB * KEPT), BF16),
-            pltpu.VMEM((2 * PAIRS, NY, 32, BS), BF16),
-            pltpu.VMEM((PAIRS, NY, 32, BS), BF16),
-            pltpu.VMEM((PAIRS, NY, 32, BS), BF16),
-            pltpu.VMEM((PAIRS, NY, 32, BS), BF16),
-            pltpu.VMEM((2 * PAIRS * NCOL, 16, 128), BF16),
+            pltpu.VMEM((NP, NY, 16, BS), BF16),
+            pltpu.VMEM((STEPS, NY, 16, BS), BF16),
+            pltpu.VMEM((STEPS, NY, 16, BS), BF16),
+            pltpu.VMEM((STEPS, NY, 16, BS), BF16),
+            pltpu.VMEM((STEPS * NCOL, 16, 128), BF16),
             pltpu.VMEM((2 * NDEP, 16, 128), BF16),
             dma((NP,)),
             dma((3,)),
@@ -309,10 +310,10 @@
             dma((2,)),
             dma((NCOL,)),
             dma((NCOL,)),
-            dma((PAIRS,)),
-            dma((PAIRS,)),
-            dma((1,)),
-            dma((PAIRS,)),
+            dma((STEPS,)),
+            dma((STEPS,)),
+            dma((1,)),
+            dma((STEPS,)),
             dma((1,)),
             dma((1,)),
         ],

time: 51.1 us -> 49.9 us (0.977)
  Pallas kernels: 48.8 us -> 47.7 us
    pallas_call x1, Pallas kernels: 48.8 us -> 47.7 us  [body(): pl.pallas_call(kernel, name='contract', out_shape=jax.ShapeDtypeStruct((2...]
where the time goes in v5:
time: 49.9 us; the launch traced here: 49.7 us
  Pallas kernels  47.7 us (96%)
  local copies, waits for them, and re-layouts  1.32 us (3%)
  between operations  0.66 us (1%)
    pallas_call x1, Pallas kernels, body(): pl.pallas_call(kernel, name='contract', out_shape=jax.ShapeDtypeStruct((2...  47.7 us
    unnamed x1, local copies, waits for them, and re-layouts  1.32 us

profile of v5, /device:TPU:1, one launch (start us, length us, event | category | flops | bytes accessed | tf_op | source)
XLA Modules:
  0.0 49.7 jit_solution(17929754282707620392)
XLA Ops:
  0.7 47.7 %contract.1 = f32[2,16,128]{2,1,0:T(8,128)} custom-call(s32[96]{0:T(128)} %atom_ref.1, s32[96]{0:T(128)} %target_ref.1, s32[96]{0:T(128)} %size_ref.1, s32[1]{0:T(128)S(6)} %copy.11.nu_ref, s32[96]{0:T(128)} %bitcast.9, bf16[12,6,256,256]{3,2,1,0:T(8,128)(2,1)} %bitcast.6, bf16[6,256,512]{2,1,0:T(8,128)(2,1)} %bitcast.7, bf16[256,128]{1,0:T(8,128)(2,1)} %occ_ref.1), custom_call_target="tpu_custom_call" | custom-call | flops 1700000000 | bytes 10000000 | tf_op jit(solution)/shard_map/contract/pallas_call | solution.py:283
  48.3 1.3 %copy.12 = f32[32,1,128]{2,1,0:T(1,128)} copy(f32[32,1,128]{2,1,0:T(1,128)} %bitcast.8) | data formatting | bytes 32768

commit v6 on v5

--- a/solution.py
+++ b/solution.py
@@ -91,7 +91,7 @@
     for copy in virt_copies:
         copy.start()
     barrier = pltpu.get_barrier_semaphore()
-    for o in (6, 5, 7, 4, 8, 3, 9, 2, 10, 1, 11):
+    for o in (5, 7, 4, 8, 3, 9, 2, 10, 1, 11):
         pl.semaphore_signal(barrier, inc=1, device_id=(row, col, deps_of[o]), device_id_type=MESH)
     for o in FAR_FIRST:
         pl.semaphore_signal(barrier, inc=1, device_id=(rows_of[o], col, dep), device_id_type=MESH)
@@ -119,7 +119,7 @@
             found += jnp.where((t >= 0) & (t < NB), t, 0)
         green_out[r] = picked[found]
 
-    pl.semaphore_wait(barrier, NDEP + NROW + NCOL - 3)
+    pl.semaphore_wait(barrier, NDEP + NROW + NCOL - 4)
     sent = []
 
     @pl.loop(0, NROW - 1)
@@ -154,6 +154,10 @@
         )
         copy.start()
         sent.append(copy)
+    before = pl.ds(pl.multiple_of(lax.rem(share + 2, 3) * SHARE, SHARE), SHARE)
+    after = pl.ds(pl.multiple_of(lax.rem(share + 1, 3) * SHARE, SHARE), SHARE)
+    arrived(green_all.at[:, before, :], share_recv.at[0])
+    arrived(green_all.at[:, after, :], share_recv.at[1])
     occ_copy.wait()
     for o in range(1, NCOL):
         copy = pltpu.make_async_remote_copy(
@@ -162,10 +166,6 @@
         )
         copy.start()
         sent.append(copy)
-    before = pl.ds(pl.multiple_of(lax.rem(share + 2, 3) * SHARE, SHARE), SHARE)
-    after = pl.ds(pl.multiple_of(lax.rem(share + 1, 3) * SHARE, SHARE), SHARE)
-    arrived(green_all.at[:, before, :], share_recv.at[0])
-    arrived(green_all.at[:, after, :], share_recv.at[1])
 
     parts = []
     for j in range(NB):

time: 49.9 us -> 49.9 us (level)
  no operation moved by 1% of the time
where the time goes in v6:
time: 49.9 us; the launch traced here: 49.7 us
  Pallas kernels  47.7 us (96%)
  local copies, waits for them, and re-layouts  1.32 us (3%)
  between operations  0.66 us (1%)
    pallas_call x1, Pallas kernels, body(): pl.pallas_call(kernel, name='contract', out_shape=jax.ShapeDtypeStruct((2...  47.7 us
    unnamed x1, local copies, waits for them, and re-layouts  1.32 us

profile of v6, /device:TPU:1, one launch (start us, length us, event | category | flops | bytes accessed | tf_op | source)
XLA Modules:
  0.0 49.7 jit_solution(16100510133514747476)
XLA Ops:
  0.7 47.7 %contract.1 = f32[2,16,128]{2,1,0:T(8,128)} custom-call(s32[96]{0:T(128)} %atom_ref.1, s32[96]{0:T(128)} %target_ref.1, s32[96]{0:T(128)} %size_ref.1, s32[1]{0:T(128)S(6)} %copy.11.nu_ref, s32[96]{0:T(128)} %bitcast.9, bf16[12,6,256,256]{3,2,1,0:T(8,128)(2,1)} %bitcast.6, bf16[6,256,512]{2,1,0:T(8,128)(2,1)} %bitcast.7, bf16[256,128]{1,0:T(8,128)(2,1)} %occ_ref.1), custom_call_target="tpu_custom_call" | custom-call | flops 1700000000 | bytes 10000000 | tf_op jit(solution)/shard_map/contract/pallas_call | solution.py:283
  48.3 1.3 %copy.12 = f32[32,1,128]{2,1,0:T(1,128)} copy(f32[32,1,128]{2,1,0:T(1,128)} %bitcast.8) | data formatting | bytes 32768
